TPU v7x, 32 devices: a whole 2x2x4 slice. The times are simulated.
32 devices in a mesh: groups: 2 (over y), tm: 4 (over z), head: 2 (over x), mp: 2 (over core).
Axes of the slice: x: 2, y: 2, z: 4, core: 2. Of those that a mesh axis runs over, the one named last changes fastest.
Arguments:
- queries: bfloat16 [2048, 2048], P(('groups', 'tm'), ('head', 'mp')), parts along dimension 0, may hold values from -6 to 6
- key_rows: bfloat16 [2048, 2048], P(('groups', 'tm'), ('head', 'mp')), parts along dimension 0, may hold values from -6 to 6
- value_rows: bfloat16 [2048, 2048], P(('groups', 'tm'), ('head', 'mp')), parts along dimension 0, may hold values from -12 to 12
- cotangent: bfloat16 [2048, 2048], P(('groups', 'tm'), ('head', 'mp')), parts along dimension 0, may hold values from -12 to 12
- block_active: int32 [16], P('groups'), parts along dimension 0, may hold values from 0 to 1
- send_counts: int32 [8, 2], P('groups'), parts along dimension 0, may hold values from 0 to 1, as said below
- block_mask: int32 [16, 8], P('groups'), parts along dimension 0, may hold values from 0 to 1, as said below
Outputs:
- attended: bfloat16 [4096, 2048], P(('groups', 'tm'), ('head', 'mp')), parts along dimension 0
- query_grad: bfloat16 [4096, 2048], P(('groups', 'tm'), ('head', 'mp')), parts along dimension 0
- key_grad: bfloat16 [2048, 2048], P(('groups', 'tm'), ('head', 'mp')), parts along dimension 0
- value_grad: bfloat16 [2048, 2048], P(('groups', 'tm'), ('head', 'mp')), parts along dimension 0
There are 2 independent parts, one for each index of `groups`. A program takes and returns all parts, laid end to end along the dimension named above; each array names one. Nothing has to cross between parts.
Inputs may be any that keep to these rules, and one draw needn't show every extreme that they name: `send_counts`: column 0 of row i counts the first blocks of shard i that go to shard i-1, column 1 its last blocks that go to shard i+1 (shard 0 follows shard 4-1); the two sum to at most 2; every block that is handed on is active. `block_mask`: the diagonal is 1.
All inputs are finite; a program needn't handle non-finite values.
Results may differ from a plain program's by a relative error of at most 0.02.
Values may be sent and summed in bfloat16 or wider, within the bound.
A program may use at most 64 MiB of HBM per device.

v0:
```python
import math
import jax
import jax.numpy as jnp
from jax import lax
from jax.sharding import PartitionSpec as P

HD = 128
BLK = 128
CAP = 1
very_low = -1e30


def extended_2(shard, sides, width):
    for axis, dim in sides:
        peers, length = (lax.axis_size(axis), shard.shape[dim])
        up = [(i, (i + 1) % peers) for i in range(peers)]
        down = [(j, i) for i, j in up]
        last = lax.slice_in_dim(shard, length - width, length, axis=dim)
        first = lax.slice_in_dim(shard, 0, width, axis=dim)
        before = lax.ppermute(last, axis, up)
        after = lax.ppermute(first, axis, down)
        shard = jnp.concatenate([before, shard, after], axis=dim)
    return shard


def pick(table, positions, extent):
    matches = positions[:, None] == jnp.arange(extent, dtype=jnp.int32)[None, :]
    return jnp.sum(jnp.where(matches, table[None, :], 0), axis=1)


def slot_layout(block_active, send_counts, block_mask, shards, own_blocks, capacity):
    slot_count = own_blocks + 2 * capacity
    all_blocks = shards * own_blocks
    places = jnp.arange(shards * slot_count, dtype=jnp.int32)
    device = places // slot_count
    slot_index = places % slot_count
    before = (device + shards - 1) % shards
    following = (device + 1) % shards
    to_left = send_counts[:, 0]
    to_right = send_counts[:, 1]
    from_before = slot_index < capacity
    from_after = slot_index >= capacity + own_blocks
    owner_shard = jnp.where(from_before, before, jnp.where(from_after, following, device))
    local_block = jnp.where(
        from_before,
        own_blocks - capacity + slot_index,
        jnp.where(from_after, slot_index - capacity - own_blocks, slot_index - capacity),
    )
    middle_ok = (local_block >= pick(to_left, device, shards)) & (
        local_block < own_blocks - pick(to_right, device, shards)
    )
    holds_record = jnp.where(
        from_before,
        slot_index >= capacity - pick(to_right, before, shards),
        jnp.where(from_after, local_block < pick(to_left, following, shards), middle_ok),
    )
    anchor = owner_shard * own_blocks + local_block
    onehot = (anchor[:, None] == jnp.arange(all_blocks, dtype=jnp.int32)[None, :]).astype(
        jnp.float32
    )
    seeing = (block_mask * block_active[None, :]).astype(jnp.float32)
    block_rows = jnp.dot(onehot, seeing, precision=lax.Precision.HIGHEST)
    active = jnp.dot(onehot, block_active.astype(jnp.float32), precision=lax.Precision.HIGHEST)
    present = jnp.where(holds_record, active, 0.0)
    return (anchor, block_rows * present[:, None], present)


def block_hot(offset, length, extent):
    blocks = (offset + jnp.arange(length, dtype=jnp.int32)) // BLK
    return (blocks[:, None] == jnp.arange(extent, dtype=jnp.int32)[None, :]).astype(jnp.bfloat16)


def sweep(update, running, pieces, offset):
    row_count = pieces[0].shape[0]
    step_rows = math.gcd(row_count, 1024)
    if step_rows == row_count:
        return update(running, pieces, offset)

    def one_turn(turn_index, carried):
        part_pieces = tuple(
            (
                lax.dynamic_slice_in_dim(member, turn_index * step_rows, step_rows, 0)
                for member in pieces
            )
        )
        return update(carried, part_pieces, offset + turn_index * step_rows)

    return lax.fori_loop(0, row_count // step_rows, one_turn, running)


def body(queries, key_rows, value_rows, cotangent, block_active, send_counts, block_mask):
    shards = lax.axis_size("tm")
    shard_index = lax.axis_index("tm")
    model_width = queries.shape[1]
    head_count = model_width // HD
    own_rows = queries.shape[0]
    own_blocks = own_rows // BLK
    all_blocks = block_active.shape[0]
    slot_count = own_blocks + 2 * CAP
    slot_rows = slot_count * BLK
    scaling = 1.0 / math.sqrt(HD)
    anchor, table, present = slot_layout(
        block_active, send_counts, block_mask, shards, own_blocks, CAP
    )
    records = jnp.concatenate([queries, cotangent], axis=1)
    extended = extended_2(records, (("tm", 0),), CAP * BLK)
    query_slots = extended[:, :model_width].reshape(slot_rows, head_count, HD)
    cotan_slots = extended[:, model_width:].reshape(slot_rows, head_count, HD)
    my_table = lax.dynamic_slice_in_dim(table, shard_index * slot_count, slot_count, 0)
    query_table = jnp.repeat(my_table, BLK, axis=0).astype(jnp.bfloat16)
    live = (
        jnp.repeat(lax.dynamic_slice_in_dim(present, shard_index * slot_count, slot_count, 0), BLK)
        > 0.5
    )
    keys_all, values_all = (
        lax.all_gather(key_rows, "tm", axis=0, tiled=True),
        lax.all_gather(value_rows, "tm", axis=0, tiled=True),
    )

    def own_scores(key_piece, offset):
        allowed = (
            lax.dot_general(
                query_table,
                block_hot(offset, key_piece.shape[0], all_blocks),
                (((1,), (1,)), ((), ())),
                preferred_element_type=jnp.float32,
            )[:, None, :]
            > 0.5
        )
        scores = (
            jnp.einsum("qhd,khd->qhk", query_slots, key_piece, preferred_element_type=jnp.float32)
            * scaling
        )
        return (allowed, scores)

    def forward(running, pieces, offset):
        peak, masses, accum = running
        key_piece = pieces[0].reshape(-1, head_count, HD)
        value_piece = pieces[1].reshape(-1, head_count, HD)
        allowed, scores = own_scores(key_piece, offset)
        new_peak = jnp.maximum(peak, jnp.max(jnp.where(allowed, scores, very_low), axis=2))
        weights = jnp.where(
            allowed, jnp.exp(jnp.where(allowed, scores - new_peak[:, :, None], 0.0)), 0.0
        )
        shrink = jnp.exp(peak - new_peak)
        masses = masses * shrink + jnp.sum(weights, axis=2)
        accum = accum * shrink[:, :, None] + jnp.einsum(
            "qhk,khd->qhd",
            weights.astype(jnp.bfloat16),
            value_piece,
            preferred_element_type=jnp.float32,
        )
        return (new_peak, masses, accum)

    initial = (
        jnp.full((slot_rows, head_count), very_low, jnp.float32),
        jnp.zeros((slot_rows, head_count), jnp.float32),
        jnp.zeros((slot_rows, head_count, HD), jnp.float32),
    )
    peak, masses, accum = sweep(forward, initial, (keys_all, values_all), 0)
    denominator = jnp.where(live[:, None], masses, 1.0)
    attended = (accum / denominator[:, :, None]).astype(jnp.bfloat16)
    log_norm = peak + jnp.log(denominator)
    deltas = jnp.sum(cotan_slots.astype(jnp.float32) * attended.astype(jnp.float32), axis=2)

    def own_gradients(key_piece, value_piece, offset):
        allowed, scores = own_scores(key_piece, offset)
        probs = jnp.where(
            allowed, jnp.exp(jnp.where(allowed, scores - log_norm[:, :, None], 0.0)), 0.0
        )
        weight_grad = jnp.einsum(
            "qhd,khd->qhk", cotan_slots, value_piece, preferred_element_type=jnp.float32
        )
        return (probs, (probs * (weight_grad - deltas[:, :, None])).astype(jnp.bfloat16))

    zero_query = jnp.zeros((slot_rows, head_count, HD), jnp.float32)

    def query_pass(query_sum, pieces, offset):
        key_piece = pieces[0].reshape(-1, head_count, HD)
        value_piece = pieces[1].reshape(-1, head_count, HD)
        probs, score_grad = own_gradients(key_piece, value_piece, offset)
        return query_sum + jnp.einsum(
            "qhk,khd->qhd", score_grad, key_piece, preferred_element_type=jnp.float32
        )

    query_sum = sweep(query_pass, zero_query, (keys_all, values_all), 0)
    own_keys = key_rows.reshape(own_rows, head_count, HD)
    own_values = value_rows.reshape(own_rows, head_count, HD)
    own_hot = block_hot(shard_index * own_rows, own_rows, all_blocks)
    slot_table = table.astype(jnp.bfloat16)
    logsum_all, delta_all = (
        lax.all_gather(log_norm, "tm", axis=0, tiled=True),
        lax.all_gather(deltas, "tm", axis=0, tiled=True),
    )

    def owner_work(running, pieces, offset):
        key_sum, value_sum = running
        query_piece, cotan_piece = pieces
        row_count = query_piece.shape[0]
        logsum_piece = lax.dynamic_slice_in_dim(logsum_all, offset, row_count, 0)
        delta_piece = lax.dynamic_slice_in_dim(delta_all, offset, row_count, 0)
        piece_table = jnp.dot(
            block_hot(offset, row_count, shards * slot_count),
            slot_table,
            preferred_element_type=jnp.float32,
        ).astype(jnp.bfloat16)
        allowed = (
            lax.dot_general(
                piece_table, own_hot, (((1,), (1,)), ((), ())), preferred_element_type=jnp.float32
            )[:, None, :]
            > 0.5
        )
        query_three = query_piece.reshape(row_count, head_count, HD)
        cotan_three = cotan_piece.reshape(row_count, head_count, HD)
        scores = (
            jnp.einsum("qhd,khd->qhk", query_three, own_keys, preferred_element_type=jnp.float32)
            * scaling
        )
        probs = jnp.where(
            allowed, jnp.exp(jnp.where(allowed, scores - logsum_piece[:, :, None], 0.0)), 0.0
        )
        weight_grad = jnp.einsum(
            "qhd,khd->qhk", cotan_three, own_values, preferred_element_type=jnp.float32
        )
        score_grad = (probs * (weight_grad - delta_piece[:, :, None])).astype(jnp.bfloat16)
        key_sum = key_sum + jnp.einsum(
            "qhk,qhd->khd", score_grad, query_three, preferred_element_type=jnp.float32
        )
        value_sum = value_sum + jnp.einsum(
            "qhk,qhd->khd",
            probs.astype(jnp.bfloat16),
            cotan_three,
            preferred_element_type=jnp.float32,
        )
        return (key_sum, value_sum)

    key_zero = jnp.zeros((own_rows, head_count, HD), jnp.float32)
    key_sum, value_sum = sweep(
        owner_work,
        (key_zero, key_zero),
        (
            lax.all_gather(query_slots.reshape(slot_rows, model_width), "tm", axis=0, tiled=True),
            lax.all_gather(cotan_slots.reshape(slot_rows, model_width), "tm", axis=0, tiled=True),
        ),
        jnp.int32(0),
    )
    key_grad = (key_sum * scaling).astype(jnp.bfloat16).reshape(own_rows, model_width)
    value_grad = value_sum.astype(jnp.bfloat16).reshape(own_rows, model_width)
    query_grad = (query_sum * scaling).astype(jnp.bfloat16).reshape(slot_rows, model_width)
    return (attended.reshape(slot_rows, model_width), query_grad, key_grad, value_grad)


def solution(mesh):
    in_specs = (
        P(("groups", "tm"), ("head", "mp")),
        P(("groups", "tm"), ("head", "mp")),
        P(("groups", "tm"), ("head", "mp")),
        P(("groups", "tm"), ("head", "mp")),
        P("groups"),
        P("groups", None),
        P("groups", None),
    )
    out_specs = (
        P(("groups", "tm"), ("head", "mp")),
        P(("groups", "tm"), ("head", "mp")),
        P(("groups", "tm"), ("head", "mp")),
        P(("groups", "tm"), ("head", "mp")),
    )
    return jax.shard_map(body, mesh=mesh, in_specs=in_specs, out_specs=out_specs, check_vma=False)
```

profile of v0, /device:TPU:0, one launch (start us, length us, event | category | flops | bytes accessed | tf_op | source)
XLA Modules:
  0.0 210.3 jit_solution(11697124278992950127)
XLA Ops:
  7.3 1.8 copy.78
  9.9 1.1 copy.76
  11.0 1.1 copy.77
  12.1 5.1 %collective-permute-start.1 = (bf16[128,1024]{0,1:T(8,128)(2,1)S(1)}, bf16[128,1024]{0,1:T(8,128)(2,1)S(1)}, u32[]{:S(2)}, u32[]{:S(2)}) collective-permute-start(bf16[128,1024]{0,1:T(8,128)(2,1)S(1)} %get-tuple-element.421), channel_id=1, source_target_pairs={{4,0},{8,4},{12,8},{0,12},{5,1},{9,5},{13,9},{1,13},{6,2},{10,6},{... | collective-permute-start | bytes 786440 | tf_op jit(solution)/shard_map/ppermute | solution.py:21
  17.2 9.6 %collective-permute-done.1 = bf16[128,1024]{0,1:T(8,128)(2,1)S(1)} collective-permute-done((bf16[128,1024]{0,1:T(8,128)(2,1)S(1)}, bf16[128,1024]{0,1:T(8,128)(2,1)S(1)}, u32[]{:S(2)}, u32[]{:S(2)}) %collective-permute-start.1) | collective-permute-done | bytes 262176 | tf_op jit(solution)/shard_map/ppermute | solution.py:21
  26.8 10.1 %collective-permute-done = bf16[128,1024]{0,1:T(8,128)(2,1)S(1)} collective-permute-done((bf16[128,1024]{0,1:T(8,128)(2,1)S(1)}, bf16[128,1024]{0,1:T(8,128)(2,1)S(1)}, u32[]{:S(2)}, u32[]{:S(2)}) %collective-permute-start) | collective-permute-done | bytes 262176 | tf_op jit(solution)/shard_map/ppermute | solution.py:20
  37.1 1.1 fusion.82
  40.9 7.4 %all-gather.5.cloned.1.call-done = bf16[1024,512]{0,1:T(8,128)(2,1)} async-done(((bf16[256,512]{0,1:T(8,128)(2,1)}), bf16[1024,512]{0,1:T(8,128)(2,1)}) %all-gather.5.cloned.1.call-update) | async-done | bytes 1048592 | tf_op jit(solution)/shard_map/all_gather | solution.py:116
  48.3 6.2 %fusion.34 = (f32[512,4]{0,1:T(4,128)S(1)}, f32[4,512,1024]{2,1,0:T(8,128)}) fusion(pred[512,1024]{1,0:T(8,128)(4,1)S(1)} %convolution_compare_fusion.1, bf16[512,4,128]{0,2,1:T(8,128)(2,1)S(1)} %bitcast.173, bf16[1024,4,128]{0,2,1:T(8,128)(2,1)} %bitcast.176), kind=kOutput, calls=%fused_computation.46 | convolution fusion | flops 543160320 | bytes 10493952 | tf_op jit(solution)/shard_map/qhd,khd->qhk/dot_general | solution.py:131
  54.5 22.5 %all-gather.7.cloned.1.call-done = bf16[1024,512]{1,0:T(8,128)(2,1)} async-done(((bf16[256,512]{1,0:T(8,128)(2,1)}), bf16[1024,512]{1,0:T(8,128)(2,1)}) %all-gather.7.cloned.1.call-update) | async-done | bytes 1048592 | tf_op jit(solution)/shard_map/all_gather | solution.py:117
  77.1 2.3 %copy.81 = bf16[1024,512]{0,1:T(8,128)(2,1)} copy(bf16[1024,512]{1,0:T(8,128)(2,1)} %all-gather.7.cloned.1.call-done) | data formatting | bytes 2097152 | tf_op jit(solution)/shard_map/all_gather | solution.py:117
  79.4 5.3 %fusion.41 = f32[512,4]{0,1:T(4,128)S(1)} fusion(f32[4,512,1024]{2,1,0:T(8,128)} %get-tuple-element.426, f32[512,4]{0,1:T(4,128)S(1)} %broadcast_maximum_fusion, pred[512,1024]{1,0:T(8,128)(4,1)S(1)} %convolution_compare_fusion.1), kind=kLoop, calls=%fused_computation.53 | loop fusion | flops 10483712 | bytes 8929280 | tf_op jit(solution)/shard_map/reduce_sum | solution.py:146
  85.3 5.0 %multiply_reduce_fusion = (f32[512,4]{0,1:T(4,128)S(1)}, bf16[512,4,128]{0,2,1:T(8,128)(2,1)}) fusion(bf16[512,1024]{0,1:T(8,128)(2,1)S(1)} %pad_maximum_fusion, f32[512,4]{0,1:T(4,128)S(1)} %get-tuple-element.413, bf16[1024,4,128]{0,2,1:T(8,128)(2,1)} %bitcast.180, f32[4,512,1024]{2,1,0:T(8,128)S(1)} %copy-done, f32[512,4]{0,1:T(4,128)S(1)} %broadcast_maximum_fusion, ...), kind=kOutput, calls=%fused_computation.69 | convolution fusion | flops 549189632 | bytes 11042816 | tf_op jit(solution)/shard_map/qhk,khd->qhd/dot_general | solution.py:147
  90.3 2.0 copy.91
  92.4 8.0 %fusion.60 = bf16[4,512,128]{1,2,0:T(8,128)(2,1)S(1)} fusion(bf16[1024,4,128]{0,2,1:T(8,128)(2,1)S(1)} %bitcast.177, f32[4,512,1024]{2,1,0:T(8,128)} %get-tuple-element.426, f32[512,4]{0,1:T(4,128)S(1)} %get-tuple-element.427, f32[512,4]{0,1:T(4,128)S(1)} %get-tuple-element.412, pred[512,1024]{1,0:T(8,128)(4,1)S(1)} %convolution_compare_fusion.1, ...), kind=kOutput, calls=%fused_computation.64 | convolution fusion | flops 1088946176 | bytes 12075008 | tf_op jit(solution)/shard_map/qhk,khd->qhd/dot_general | solution.py:182
  100.4 1.0 copy.92
  101.4 13.4 %all_gather.21 = f32[2048,4]{0,1:T(4,128)S(1)} all-gather(f32[512,4]{0,1:T(4,128)S(1)} %get-tuple-element.412), channel_id=1, replica_groups=mesh['groups'=2,'tm'=4,'head'=2,'mp'=2] {'tm'}, dimensions={0}, use_global_device_ids=true | all-gather | bytes 40960 | tf_op jit(solution)/shard_map/all_gather | solution.py:192
  114.7 13.3 %all_gather.23 = f32[2048,4]{0,1:T(4,128)S(1)} all-gather(f32[512,4]{0,1:T(4,128)S(1)} %get-tuple-element.427), channel_id=1, replica_groups=mesh['groups'=2,'tm'=4,'head'=2,'mp'=2] {'tm'}, dimensions={0}, use_global_device_ids=true | all-gather | bytes 40960 | tf_op jit(solution)/shard_map/all_gather | solution.py:193
  128.0 43.1 %all-gather.11.cloned.1.call-done = bf16[2048,512]{0,1:T(8,128)(2,1)} async-done(((bf16[512,512]{0,1:T(8,128)(2,1)}), bf16[2048,512]{0,1:T(8,128)(2,1)}) %all-gather.11.cloned.1.call-update) | async-done | bytes 2097168 | tf_op jit(solution)/shard_map/all_gather | solution.py:243
  171.1 28.8 %while.18 = (s32[]{:T(128)}, f32[256,4,128]{0,2,1:T(8,128)}, f32[256,4,128]{0,2,1:T(8,128)}, bf16[2048,512]{0,1:T(8,128)(2,1)}, bf16[16,8]{0,1:T(8,128)(2,1)S(1)...) while((s32[]{:T(128)}, f32[256,4,128]{0,2,1:T(8,128)}, ...), condition=%wide.region_8.9_spmd.clone, body=%wide.region_7.8_spmd.clone.sunk | while | flops 1091612672 | bytes 32892488 | solution.py:88
  171.1 1.7 constant_dynamic-slice_fusion.6
  172.9 2.7 %fusion.119 = f32[4,1024,256]{2,1,0:T(8,128)} fusion(bf16[1024,4,128]{0,2,1:T(8,128)(2,1)S(1)} %bitcast.169, bf16[256,4,128]{2,0,1:T(8,128)(2,1)S(1)} %get-tuple-element.541), kind=kOutput, calls=%fused_computation.134.clone.1 | convolution fusion | flops 268435456 | bytes 5505024 | tf_op jit(solution)/shard_map/while/body/eval_jaxpr/qhd,khd->qhk/dot_general | solution.py:216
  175.6 1.3 convolution_compare_fusion.3
  176.9 4.5 %fusion.120 = f32[256,4,128]{0,2,1:T(8,128)S(1)} fusion(bf16[1024,4,128]{0,2,1:T(8,128)(2,1)S(1)} %bitcast.170, f32[4,1024,256]{2,1,0:T(8,128)} %fusion.119, bf16[1024,4,128]{0,2,1:T(8,128)(2,1)S(1)} %bitcast.171, bf16[256,4,128]{2,0,1:T(8,128)(2,1)} %get-tuple-element.544, f32[1024,4]{0,1:T(4,128)S(1)} %get-tuple-element.504, ...), kind=kOutput, calls=%fused_computation.16.clone.1 | convolution fusion | flops 544473088 | bytes 7897089 | tf_op jit(solution)/shard_map/while/body/eval_jaxpr/qhk,qhd->khd/dot_general | solution.py:226
  181.5 3.2 %fusion.121 = f32[256,4,128]{0,2,1:T(8,128)S(1)} fusion(bf16[1024,4,128]{0,2,1:T(8,128)(2,1)S(1)} %bitcast.172, f32[4,1024,256]{2,1,0:T(8,128)} %fusion.119, f32[1024,4]{0,1:T(4,128)S(1)} %get-tuple-element.505, pred[1024,256]{1,0:T(8,128)(4,1)} %convolution_compare_fusion.3, f32[256,4,128]{0,2,1:T(8,128)S(1)} %copy-done.8, pred[]{:T(512)S(6)} %compare.53), kind=kOutput, calls=%fused_computation.15.clone.1 | convolution fusion | flops 273940480 | bytes 6569985 | tf_op jit(solution)/shard_map/while/body/eval_jaxpr/qhk,qhd->khd/dot_general | solution.py:229
  185.5 1.7 constant_dynamic-slice_fusion.6
  187.3 2.7 %fusion.119 = f32[4,1024,256]{2,1,0:T(8,128)} fusion(bf16[1024,4,128]{0,2,1:T(8,128)(2,1)S(1)} %bitcast.169, bf16[256,4,128]{2,0,1:T(8,128)(2,1)S(1)} %get-tuple-element.541), kind=kOutput, calls=%fused_computation.134.clone.1 | convolution fusion | flops 268435456 | bytes 5505024 | tf_op jit(solution)/shard_map/while/body/eval_jaxpr/qhd,khd->qhk/dot_general | solution.py:216
  190.0 1.3 convolution_compare_fusion.3
  191.3 4.5 %fusion.120 = f32[256,4,128]{0,2,1:T(8,128)S(1)} fusion(bf16[1024,4,128]{0,2,1:T(8,128)(2,1)S(1)} %bitcast.170, f32[4,1024,256]{2,1,0:T(8,128)} %fusion.119, bf16[1024,4,128]{0,2,1:T(8,128)(2,1)S(1)} %bitcast.171, bf16[256,4,128]{2,0,1:T(8,128)(2,1)} %get-tuple-element.544, f32[1024,4]{0,1:T(4,128)S(1)} %get-tuple-element.504, ...), kind=kOutput, calls=%fused_computation.16.clone.1 | convolution fusion | flops 544473088 | bytes 7897089 | tf_op jit(solution)/shard_map/while/body/eval_jaxpr/qhk,qhd->khd/dot_general | solution.py:226
  195.9 3.2 %fusion.121 = f32[256,4,128]{0,2,1:T(8,128)S(1)} fusion(bf16[1024,4,128]{0,2,1:T(8,128)(2,1)S(1)} %bitcast.172, f32[4,1024,256]{2,1,0:T(8,128)} %fusion.119, f32[1024,4]{0,1:T(4,128)S(1)} %get-tuple-element.505, pred[1024,256]{1,0:T(8,128)(4,1)} %convolution_compare_fusion.3, f32[256,4,128]{0,2,1:T(8,128)S(1)} %copy-done.8, pred[]{:T(512)S(6)} %compare.53), kind=kOutput, calls=%fused_computation.15.clone.1 | convolution fusion | flops 273940480 | bytes 6569985 | tf_op jit(solution)/shard_map/while/body/eval_jaxpr/qhk,qhd->khd/dot_general | solution.py:229
  199.9 1.1 multiply_convert_fusion
  201.9 1.1 convert_element_type.96
  (74 shorter events, 7.6 us)
Async XLA Ops:
  7.2 31.1 %copy-start.5 = (bf16[256,512]{1,0:T(8,128)(2,1)S(1)}, bf16[256,512]{1,0:T(8,128)(2,1)}, u32[]{:S(2)}) copy-start(bf16[256,512]{1,0:T(8,128)(2,1)} %param.11) | copy-start | bytes 786436
  7.2 31.3 %copy-start.10 = (s32[4,2]{0,1:T(2,128)S(1)}, s32[4,2]{0,1:T(2,128)}, u32[]{:S(2)}) copy-start(s32[4,2]{0,1:T(2,128)} %param.14) | copy-start | bytes 100
  7.2 31.4 %copy-start.12 = (s32[8]{0:T(128)S(1)}, s32[8]{0:T(128)}, u32[]{:S(2)}) copy-start(s32[8]{0:T(128)} %param.13) | copy-start | bytes 100
  7.2 31.6 %copy-start.11 = (s32[8,8]{1,0:T(8,128)S(1)}, s32[8,8]{1,0:T(8,128)}, u32[]{:S(2)}) copy-start(s32[8,8]{1,0:T(8,128)} %param.15) | copy-start | bytes 772
  7.2 41.1 %all-gather.5.cloned.1.call-start = ((), (), s32[]{:S(2)}) async-start(), calls=%async_computation | async-start | bytes 1310720 | tf_op jit(solution)/shard_map/all_gather | solution.py:116
  9.1 30.0 %copy-start.2 = (bf16[256,512]{0,1:T(8,128)(2,1)S(1)}, bf16[256,512]{0,1:T(8,128)(2,1)}, u32[]{:S(2)}) copy-start(bf16[256,512]{0,1:T(8,128)(2,1)} %copy.78) | copy-start | bytes 786436
  9.1 67.9 %all-gather.7.cloned.1.call-start = ((), (), s32[]{:S(2)}) async-start(), calls=%async_computation.1 | async-start | bytes 1310720 | tf_op jit(solution)/shard_map/all_gather | solution.py:117
  9.9 118.2 %all-gather.9.cloned.1.call-start = ((), (), s32[]{:S(2)}) async-start(), calls=%async_computation.2 | async-start | bytes 2621440 | tf_op jit(solution)/shard_map/all_gather | solution.py:242
  12.1 14.7 %collective-permute-start.1 = (bf16[128,1024]{0,1:T(8,128)(2,1)S(1)}, bf16[128,1024]{0,1:T(8,128)(2,1)S(1)}, u32[]{:S(2)}, u32[]{:S(2)}) collective-permute-start(bf16[128,1024]{0,1:T(8,128)(2,1)S(1)} %get-tuple-element.421), channel_id=1, source_target_pairs={{4,0},{8,4},{12,8},{0,12},{5,1},{9,5},{13,9},{1,13},{6,2},{10,6},{... | collective-permute-start | bytes 786440 | tf_op jit(solution)/shard_map/ppermute | solution.py:21
  17.2 19.7 %collective-permute-start = (bf16[128,1024]{0,1:T(8,128)(2,1)S(1)}, bf16[128,1024]{0,1:T(8,128)(2,1)S(1)}, u32[]{:S(2)}, u32[]{:S(2)}) collective-permute-start(bf16[128,1024]{0,1:T(8,128)(2,1)S(1)} %get-tuple-element.420), channel_id=1, source_target_pairs={{0,4},{4,8},{8,12},{12,0},{1,5},{5,9},{9,13},{13,1},{2,6},{6,10},{... | collective-permute-start | bytes 786440 | tf_op jit(solution)/shard_map/ppermute | solution.py:20
  38.1 10.1 %copy-start.1 = (bf16[512,512]{0,1:T(8,128)(2,1)S(1)}, bf16[512,512]{0,1:T(8,128)(2,1)}, u32[]{:S(2)}) copy-start(bf16[512,512]{0,1:T(8,128)(2,1)} %get-tuple-element.419) | copy-start | bytes 1572868
  38.2 133.0 %all-gather.11.cloned.1.call-start = ((), (), s32[]{:S(2)}) async-start(), calls=%async_computation.3 | async-start | bytes 2621440 | tf_op jit(solution)/shard_map/all_gather | solution.py:243
  79.4 6.0 %copy-start = (f32[4,512,1024]{2,1,0:T(8,128)S(1)}, f32[4,512,1024]{2,1,0:T(8,128)}, u32[]{:S(2)}) copy-start(f32[4,512,1024]{2,1,0:T(8,128)} %get-tuple-element.426) | copy-start | bytes 25165828
  85.3 7.1 %copy-start.3 = (bf16[512,512]{0,1:T(8,128)(2,1)S(1)}, bf16[512,512]{0,1:T(8,128)(2,1)}, u32[]{:S(2)}) copy-start(bf16[512,512]{0,1:T(8,128)(2,1)} %get-tuple-element.418) | copy-start | bytes 1572868
  85.3 7.1 %copy-start.4 = (bf16[1024,512]{0,1:T(8,128)(2,1)S(1)}, bf16[1024,512]{0,1:T(8,128)(2,1)}, u32[]{:S(2)}) copy-start(bf16[1024,512]{0,1:T(8,128)(2,1)} %all-gather.5.cloned.1.call-done) | copy-start | bytes 3145732
  172.8 4.0 %copy-start.6 = (f32[256,4,128]{0,2,1:T(8,128)S(1)}, f32[256,4,128]{0,2,1:T(8,128)}, u32[]{:S(2)}) copy-start(f32[256,4,128]{0,2,1:T(8,128)} %get-tuple-element.522) | copy-start | bytes 1572868 | tf_op jit(solution)/shard_map/while
  176.9 4.5 %copy-start.8 = (f32[256,4,128]{0,2,1:T(8,128)S(1)}, f32[256,4,128]{0,2,1:T(8,128)}, u32[]{:S(2)}) copy-start(f32[256,4,128]{0,2,1:T(8,128)} %get-tuple-element.523) | copy-start | bytes 1572868 | tf_op jit(solution)/shard_map/while
  181.4 3.3 %copy-start.7 = (f32[256,4,128]{0,2,1:T(8,128)}, f32[256,4,128]{0,2,1:T(8,128)S(1)}, u32[]{:S(2)}) copy-start(f32[256,4,128]{0,2,1:T(8,128)S(1)} %fusion.120) | copy-start | bytes 1572868 | tf_op jit(solution)/shard_map/while
  184.7 0.8 copy-start.9
  187.3 4.0 %copy-start.6 = (f32[256,4,128]{0,2,1:T(8,128)S(1)}, f32[256,4,128]{0,2,1:T(8,128)}, u32[]{:S(2)}) copy-start(f32[256,4,128]{0,2,1:T(8,128)} %get-tuple-element.522) | copy-start | bytes 1572868 | tf_op jit(solution)/shard_map/while
  191.3 4.5 %copy-start.8 = (f32[256,4,128]{0,2,1:T(8,128)S(1)}, f32[256,4,128]{0,2,1:T(8,128)}, u32[]{:S(2)}) copy-start(f32[256,4,128]{0,2,1:T(8,128)} %get-tuple-element.523) | copy-start | bytes 1572868 | tf_op jit(solution)/shard_map/while
  195.8 3.3 %copy-start.7 = (f32[256,4,128]{0,2,1:T(8,128)}, f32[256,4,128]{0,2,1:T(8,128)S(1)}, u32[]{:S(2)}) copy-start(f32[256,4,128]{0,2,1:T(8,128)S(1)} %fusion.120) | copy-start | bytes 1572868 | tf_op jit(solution)/shard_map/while
  199.1 0.8 copy-start.9
Sparse Core Ops, SparseCore 0:
  10.2 38.0 all-gather.4
  49.9 27.1 all-gather.6
  78.6 46.3 all-gather.8
  126.5 44.6 all-gather.10
where the time goes:
time: 211 us; the launch traced here: 210 us
  waiting for transfers between devices  93.5 us (44%)
  matrix products  43.7 us (21%)
  blocking collectives  26.7 us (13%)
  local copies, waits for them, and re-layouts  19.2 us (9%)
  between operations  14 us (7%)
  other arithmetic  7.86 us (4%)
  starting transfers between devices  5.26 us (2%)
    all_gather x1, waiting for transfers between devices, body(): lax.all_gather(cotan_slots.reshape(slot_rows, model_width), 'tm', axis=0,...  43.1 us
    all_gather x1, waiting for transfers between devices, body(): lax.all_gather(value_rows, 'tm', axis=0, tiled=True)  22.5 us
    all_gather x1, blocking collectives, body(): lax.all_gather(log_norm, 'tm', axis=0, tiled=True)  13.4 us
    all_gather x1, blocking collectives, body(): lax.all_gather(deltas, 'tm', axis=0, tiled=True)  13.3 us
    ppermute x1, waiting for transfers between devices, extended_2(): before = lax.ppermute(last, axis, up)  10.1 us
    ppermute x1, waiting for transfers between devices, extended_2(): after = lax.ppermute(first, axis, down)  9.6 us
    dot_general x2, matrix products, owner_work(): jnp.einsum('qhk,qhd->khd', score_grad, query_three, preferred_element_typ...  9.05 us
    unnamed x27, local copies, waits for them, and re-layouts  8.95 us
  transfers between devices with their start and end apart: 6, of which 5 were waited for; matrix products, arithmetic and copies ran while one was open for 17% of the time, Pallas kernels for 0%

commit v1 on v0

--- a/solution.py
+++ b/solution.py
@@ -8,6 +8,19 @@
 BLK = 128
 CAP = 1
 very_low = -1e30
+
+
+def collect(array, axis, dim):
+    ways = lax.axis_size(axis)
+    up = [(d, (d + 1) % ways) for d in range(ways)]
+    down = [(d, (d - 1) % ways) for d in range(ways)]
+    earlier, later = ([array], [array])
+    for _ in range(ways // 2):
+        earlier.append(lax.ppermute(earlier[-1], axis, up))
+    for _ in range((ways - 1) // 2):
+        later.append(lax.ppermute(later[-1], axis, down))
+    line = jnp.concatenate([*earlier[::-1], *later[1:]], axis=dim)
+    return jnp.roll(line, (lax.axis_index(axis) - ways // 2) * array.shape[dim], axis=dim)
 
 
 def extended_2(shard, sides, width):
@@ -114,7 +127,7 @@
     )
     keys_all, values_all = (
         lax.all_gather(key_rows, "tm", axis=0, tiled=True),
-        lax.all_gather(value_rows, "tm", axis=0, tiled=True),
+        collect(value_rows, "tm", 0),
     )
 
     def own_scores(key_piece, offset):

time: 211 us -> 188 us (0.89)
  waiting for transfers between devices: 93.5 us -> 73.9 us
  starting transfers between devices: 5.26 us -> 12.3 us
  other arithmetic: 7.86 us -> 3.55 us
  matrix products: 43.7 us -> 39.7 us
    all_gather x1 -> x0, waiting for transfers between devices: 22.5 us -> none  [body(): lax.all_gather(value_rows, 'tm', axis=0, tiled=True)]
    ppermute x0 -> x3, waiting for transfers between devices: none -> 17.6 us  [the longest x2 17.6 us: collect(): earlier.append(lax.ppermute(earlier[-1], axis, up))]
    all_gather x1, waiting for transfers between devices: 7.42 us -> 0.01 us  [body(): lax.all_gather(key_rows, 'tm', axis=0, tiled=True)]
    ppermute x0 -> x3, starting transfers between devices: none -> 7.11 us  [the longest x2 5.75 us: collect(): earlier.append(lax.ppermute(earlier[-1], axis, up))]
    all_gather x1, waiting for transfers between devices: 43.1 us -> 37.2 us  [body(): lax.all_gather(cotan_slots.reshape(slot_rows, model_width), 'tm', axis=0,...]
    dot_general x1, matrix products: 6.24 us -> 3.17 us  [own_scores(): jnp.einsum('qhd,khd->qhk', query_slots, key_piece, preferred_element_type...]
    all_gather x1 -> x0, local copies, waits for them, and re-layouts: 2.3 us -> none  [body(): lax.all_gather(value_rows, 'tm', axis=0, tiled=True)]
    reduce_sum x1, other arithmetic: 5.31 us -> 3.08 us  [forward(): masses = masses * shrink + jnp.sum(weights, axis=2)]
  transfers between devices with their start and end apart: 6 -> 8, of which waited for: 5 -> 5; matrix products, arithmetic and copies ran while one was open for 17% -> 16% of each run, Pallas kernels for 0% -> 0%
where the time goes in v1:
time: 188 us
  waiting for transfers between devices  73.9 us (39%)
  matrix products  39.7 us (21%)
  blocking collectives  26.7 us (14%)
  local copies, waits for them, and re-layouts  17.3 us (9%)
  between operations  14.1 us (8%)
  starting transfers between devices  12.3 us (7%)
  other arithmetic  3.55 us (2%)
    all_gather x1, waiting for transfers between devices, body(): lax.all_gather(cotan_slots.reshape(slot_rows, model_width), 'tm', axis=0,...  37.2 us
    ppermute x2, waiting for transfers between devices, collect(): earlier.append(lax.ppermute(earlier[-1], axis, up))  17.6 us
    all_gather x1, blocking collectives, body(): lax.all_gather(log_norm, 'tm', axis=0, tiled=True)  13.4 us
    all_gather x1, blocking collectives, body(): lax.all_gather(deltas, 'tm', axis=0, tiled=True)  13.3 us
    ppermute x1, waiting for transfers between devices, extended_2(): before = lax.ppermute(last, axis, up)  10.1 us
    unnamed x40, local copies, waits for them, and re-layouts  9.61 us
    dot_general x2, matrix products, owner_work(): jnp.einsum('qhk,qhd->khd', score_grad, query_three, preferred_element_typ...  8.93 us
    dot_general x1, matrix products, query_pass(): jnp.einsum('qhk,khd->qhd', score_grad, key_piece, preferred_element_type=...  8.87 us
  transfers between devices with their start and end apart: 8, of which 5 were waited for; matrix products, arithmetic and copies ran while one was open for 16% of the time, Pallas kernels for 0%

profile of v1, /device:TPU:0, one launch (start us, length us, event | category | flops | bytes accessed | tf_op | source)
XLA Modules:
  0.0 187.6 jit_solution(10985440433408091893)
XLA Ops:
  7.3 1.8 copy.80
  9.2 1.1 copy.78
  10.2 1.1 copy.79
  11.4 5.1 %collective-permute-start.1 = (bf16[128,1024]{0,1:T(8,128)(2,1)S(1)}, bf16[128,1024]{0,1:T(8,128)(2,1)S(1)}, u32[]{:S(2)}, u32[]{:S(2)}) collective-permute-start(bf16[128,1024]{0,1:T(8,128)(2,1)S(1)} %get-tuple-element.421), channel_id=1, source_target_pairs={{4,0},{8,4},{12,8},{0,12},{5,1},{9,5},{13,9},{1,13},{6,2},{10,6},{... | collective-permute-start | bytes 786440 | tf_op jit(solution)/shard_map/ppermute | solution.py:34
  16.5 8.8 %collective-permute-done.1 = bf16[128,1024]{0,1:T(8,128)(2,1)S(1)} collective-permute-done((bf16[128,1024]{0,1:T(8,128)(2,1)S(1)}, bf16[128,1024]{0,1:T(8,128)(2,1)S(1)}, u32[]{:S(2)}, u32[]{:S(2)}) %collective-permute-start.1) | collective-permute-done | bytes 262176 | tf_op jit(solution)/shard_map/ppermute | solution.py:34
  25.3 10.1 %collective-permute-done = bf16[128,1024]{0,1:T(8,128)(2,1)S(1)} collective-permute-done((bf16[128,1024]{0,1:T(8,128)(2,1)S(1)}, bf16[128,1024]{0,1:T(8,128)(2,1)S(1)}, u32[]{:S(2)}, u32[]{:S(2)}) %collective-permute-start) | collective-permute-done | bytes 262176 | tf_op jit(solution)/shard_map/ppermute | solution.py:33
  36.7 2.5 %collective-permute-start.2 = (bf16[256,512]{1,0:T(8,128)(2,1)S(1)}, bf16[256,512]{1,0:T(8,128)(2,1)S(1)}, u32[]{:S(2)}, u32[]{:S(2)}) collective-permute-start(bf16[256,512]{1,0:T(8,128)(2,1)S(1)} %copy-done.2), channel_id=1, source_target_pairs={{0,4},{4,8},{8,12},{12,0},{1,5},{5,9},{9,13},{13,1},{2,6},{6,10},{... | collective-permute-start | bytes 786440 | tf_op jit(solution)/shard_map/ppermute | solution.py:19
  39.3 1.4 collective-permute-start.4
  41.3 12.0 %collective-permute-done.2 = bf16[256,512]{1,0:T(8,128)(2,1)S(1)} collective-permute-done((bf16[256,512]{1,0:T(8,128)(2,1)S(1)}, bf16[256,512]{1,0:T(8,128)(2,1)S(1)}, u32[]{:S(2)}, u32[]{:S(2)}) %collective-permute-start.2) | collective-permute-done | bytes 262176 | tf_op jit(solution)/shard_map/ppermute | solution.py:19
  53.3 3.2 %collective-permute-start.3 = (bf16[256,512]{1,0:T(8,128)(2,1)S(1)}, bf16[256,512]{1,0:T(8,128)(2,1)S(1)}, u32[]{:S(2)}, u32[]{:S(2)}) collective-permute-start(bf16[256,512]{1,0:T(8,128)(2,1)S(1)} %collective-permute-done.2), channel_id=1, source_target_pairs={{0,4},{4,8},{8,12},{12,0},{1,5},{5,9},{9,13},{13,1},{2,6},{6,10},{... | collective-permute-start | bytes 786440 | tf_op jit(solution)/shard_map/ppermute | solution.py:19
  58.5 5.6 %collective-permute-done.3 = bf16[256,512]{1,0:T(8,128)(2,1)S(1)} collective-permute-done((bf16[256,512]{1,0:T(8,128)(2,1)S(1)}, bf16[256,512]{1,0:T(8,128)(2,1)S(1)}, u32[]{:S(2)}, u32[]{:S(2)}) %collective-permute-start.3) | collective-permute-done | bytes 262176 | tf_op jit(solution)/shard_map/ppermute | solution.py:19
  64.4 1.3 copy.83
  65.8 3.2 %fusion.34 = (f32[512,4]{0,1:T(4,128)S(1)}, f32[4,512,1024]{2,1,0:T(8,128)S(1)}) fusion(pred[512,1024]{1,0:T(8,128)(4,1)S(1)} %convolution_compare_fusion.1, bf16[512,4,128]{0,2,1:T(8,128)(2,1)S(1)} %bitcast.173, bf16[1024,4,128]{0,2,1:T(8,128)(2,1)} %bitcast.176), kind=kOutput, calls=%fused_computation.46 | convolution fusion | flops 543160320 | bytes 10493952 | tf_op jit(solution)/shard_map/qhd,khd->qhk/dot_general | solution.py:144
  69.0 3.1 %fusion.41 = f32[512,4]{0,1:T(4,128)S(1)} fusion(f32[4,512,1024]{2,1,0:T(8,128)S(1)} %get-tuple-element.426, f32[512,4]{0,1:T(4,128)S(1)} %broadcast_maximum_fusion, pred[512,1024]{1,0:T(8,128)(4,1)S(1)} %convolution_compare_fusion.1), kind=kLoop, calls=%fused_computation.53 | loop fusion | flops 10483712 | bytes 8929280 | tf_op jit(solution)/shard_map/reduce_sum | solution.py:159
  72.2 3.6 %multiply_reduce_fusion = (f32[512,4]{0,1:T(4,128)S(1)}, bf16[512,4,128]{0,2,1:T(8,128)(2,1)}) fusion(bf16[512,1024]{0,1:T(8,128)(2,1)S(1)} %pad_maximum_fusion, f32[512,4]{0,1:T(4,128)S(1)} %get-tuple-element.413, bf16[1024,4,128]{0,2,1:T(8,128)(2,1)S(1)} %bitcast.181, f32[4,512,1024]{2,1,0:T(8,128)S(1)} %get-tuple-element.426, ...), kind=kOutput, calls=%fused_computation.69 | convolution fusion | flops 549189632 | bytes 11042816 | tf_op jit(solution)/shard_map/qhk,khd->qhd/dot_general | solution.py:160
  75.8 2.1 %copy.94 = bf16[512,512]{1,0:T(8,128)(2,1)} copy(bf16[512,512]{0,1:T(8,128)(2,1)} %bitcast.183) | data formatting | bytes 1048576
  77.9 8.9 %fusion.60 = bf16[4,512,128]{1,2,0:T(8,128)(2,1)} fusion(bf16[1024,4,128]{0,2,1:T(8,128)(2,1)S(1)} %bitcast.177, f32[4,512,1024]{2,1,0:T(8,128)} %copy-done, f32[512,4]{0,1:T(4,128)S(1)} %get-tuple-element.427, f32[512,4]{0,1:T(4,128)S(1)} %get-tuple-element.412, pred[512,1024]{1,0:T(8,128)(4,1)S(1)} %convolution_compare_fusion.1, ...), kind=kOutput, calls=%fused_computation.64 | convolution fusion | flops 1088946176 | bytes 12075008 | tf_op jit(solution)/shard_map/qhk,khd->qhd/dot_general | solution.py:195
  86.7 2.1 %copy.95 = bf16[512,512]{1,0:T(8,128)(2,1)} copy(bf16[512,512]{0,1:T(8,128)(2,1)} %bitcast.184) | data formatting | bytes 1048576
  88.8 13.4 %all_gather.17 = f32[2048,4]{0,1:T(4,128)S(1)} all-gather(f32[512,4]{0,1:T(4,128)S(1)} %get-tuple-element.412), channel_id=1, replica_groups=mesh['groups'=2,'tm'=4,'head'=2,'mp'=2] {'tm'}, dimensions={0}, use_global_device_ids=true | all-gather | bytes 40960 | tf_op jit(solution)/shard_map/all_gather | solution.py:205
  102.2 13.3 %all_gather.19 = f32[2048,4]{0,1:T(4,128)S(1)} all-gather(f32[512,4]{0,1:T(4,128)S(1)} %get-tuple-element.427), channel_id=1, replica_groups=mesh['groups'=2,'tm'=4,'head'=2,'mp'=2] {'tm'}, dimensions={0}, use_global_device_ids=true | all-gather | bytes 40960 | tf_op jit(solution)/shard_map/all_gather | solution.py:206
  115.5 37.2 %all-gather.8.cloned.1.call-done = bf16[2048,512]{0,1:T(8,128)(2,1)} async-done(((bf16[512,512]{0,1:T(8,128)(2,1)}), bf16[2048,512]{0,1:T(8,128)(2,1)}) %all-gather.8.cloned.1.call-update) | async-done | bytes 2097168 | tf_op jit(solution)/shard_map/all_gather | solution.py:256
  152.7 26.6 %while.18 = (s32[]{:T(128)}, f32[256,4,128]{0,2,1:T(8,128)S(1)}, f32[256,4,128]{0,2,1:T(8,128)S(1)}, bf16[2048,512]{0,1:T(8,128)(2,1)}, bf16[16,8]{0,1:T(8,128)(...) while((s32[]{:T(128)}, f32[256,4,128]{0,2,1:T(8,128)S(1)}, ...), condition=%wide.region_8.9_spmd.clone, body=%wide.region_7.8_spmd.clone.sunk | while | flops 1091612672 | bytes 24503768 | solution.py:101
  152.7 1.7 constant_dynamic-slice_fusion.7
  154.4 2.7 %fusion.119 = f32[4,1024,256]{2,1,0:T(8,128)} fusion(bf16[1024,4,128]{0,2,1:T(8,128)(2,1)S(1)} %bitcast.169, bf16[256,4,128]{2,0,1:T(8,128)(2,1)S(1)} %get-tuple-element.543), kind=kOutput, calls=%fused_computation.143.clone.1 | convolution fusion | flops 268435456 | bytes 5505024 | tf_op jit(solution)/shard_map/while/body/eval_jaxpr/qhd,khd->qhk/dot_general | solution.py:229
  157.1 1.3 convolution_compare_fusion.3
  158.4 4.5 %fusion.120 = f32[256,4,128]{0,2,1:T(8,128)S(1)} fusion(bf16[1024,4,128]{0,2,1:T(8,128)(2,1)S(1)} %bitcast.170, f32[4,1024,256]{2,1,0:T(8,128)} %fusion.119, bf16[1024,4,128]{0,2,1:T(8,128)(2,1)S(1)} %bitcast.171, bf16[256,4,128]{2,0,1:T(8,128)(2,1)} %get-tuple-element.546, f32[1024,4]{0,1:T(4,128)S(1)} %get-tuple-element.506, ...), kind=kOutput, calls=%fused_computation.16.clone.1 | convolution fusion | flops 544473088 | bytes 7897089 | tf_op jit(solution)/shard_map/while/body/eval_jaxpr/qhk,qhd->khd/dot_general | solution.py:239
  162.9 3.1 %fusion.121 = f32[256,4,128]{0,2,1:T(8,128)S(1)} fusion(bf16[1024,4,128]{0,2,1:T(8,128)(2,1)S(1)} %bitcast.172, f32[4,1024,256]{2,1,0:T(8,128)} %fusion.119, f32[1024,4]{0,1:T(4,128)S(1)} %get-tuple-element.507, pred[1024,256]{1,0:T(8,128)(4,1)} %convolution_compare_fusion.3, f32[256,4,128]{0,2,1:T(8,128)S(1)} %get-tuple-element.525, pred[]{:T(512)S(6)} %compare.54), kind=kOutput, calls=%fused_computation.15.clone.1 | convolution fusion | flops 273940480 | bytes 6569985 | tf_op jit(solution)/shard_map/while/body/eval_jaxpr/qhk,qhd->khd/dot_general | solution.py:242
  166.0 1.7 constant_dynamic-slice_fusion.7
  167.7 2.7 %fusion.119 = f32[4,1024,256]{2,1,0:T(8,128)} fusion(bf16[1024,4,128]{0,2,1:T(8,128)(2,1)S(1)} %bitcast.169, bf16[256,4,128]{2,0,1:T(8,128)(2,1)S(1)} %get-tuple-element.543), kind=kOutput, calls=%fused_computation.143.clone.1 | convolution fusion | flops 268435456 | bytes 5505024 | tf_op jit(solution)/shard_map/while/body/eval_jaxpr/qhd,khd->qhk/dot_general | solution.py:229
  170.5 1.3 convolution_compare_fusion.3
  171.8 4.5 %fusion.120 = f32[256,4,128]{0,2,1:T(8,128)S(1)} fusion(bf16[1024,4,128]{0,2,1:T(8,128)(2,1)S(1)} %bitcast.170, f32[4,1024,256]{2,1,0:T(8,128)} %fusion.119, bf16[1024,4,128]{0,2,1:T(8,128)(2,1)S(1)} %bitcast.171, bf16[256,4,128]{2,0,1:T(8,128)(2,1)} %get-tuple-element.546, f32[1024,4]{0,1:T(4,128)S(1)} %get-tuple-element.506, ...), kind=kOutput, calls=%fused_computation.16.clone.1 | convolution fusion | flops 544473088 | bytes 7897089 | tf_op jit(solution)/shard_map/while/body/eval_jaxpr/qhk,qhd->khd/dot_general | solution.py:239
  176.3 3.1 %fusion.121 = f32[256,4,128]{0,2,1:T(8,128)S(1)} fusion(bf16[1024,4,128]{0,2,1:T(8,128)(2,1)S(1)} %bitcast.172, f32[4,1024,256]{2,1,0:T(8,128)} %fusion.119, f32[1024,4]{0,1:T(4,128)S(1)} %get-tuple-element.507, pred[1024,256]{1,0:T(8,128)(4,1)} %convolution_compare_fusion.3, f32[256,4,128]{0,2,1:T(8,128)S(1)} %get-tuple-element.525, pred[]{:T(512)S(6)} %compare.54), kind=kOutput, calls=%fused_computation.15.clone.1 | convolution fusion | flops 273940480 | bytes 6569985 | tf_op jit(solution)/shard_map/while/body/eval_jaxpr/qhk,qhd->khd/dot_general | solution.py:242
  (75 shorter events, 6.1 us)
Async XLA Ops:
  7.2 29.6 %copy-start.2 = (bf16[256,512]{1,0:T(8,128)(2,1)S(1)}, bf16[256,512]{1,0:T(8,128)(2,1)}, u32[]{:S(2)}) copy-start(bf16[256,512]{1,0:T(8,128)(2,1)} %param.11) | copy-start | bytes 786436
  7.2 33.5 %copy-start.9 = (s32[4,2]{0,1:T(2,128)S(1)}, s32[4,2]{0,1:T(2,128)}, u32[]{:S(2)}) copy-start(s32[4,2]{0,1:T(2,128)} %param.14) | copy-start | bytes 100
  7.2 33.6 %copy-start.11 = (s32[8]{0:T(128)S(1)}, s32[8]{0:T(128)}, u32[]{:S(2)}) copy-start(s32[8]{0:T(128)} %param.13) | copy-start | bytes 100
  7.2 33.7 %copy-start.10 = (s32[8,8]{1,0:T(8,128)S(1)}, s32[8,8]{1,0:T(8,128)}, u32[]{:S(2)}) copy-start(s32[8,8]{1,0:T(8,128)} %param.15) | copy-start | bytes 772
  7.2 58.5 %all-gather.4.cloned.1.call-start = ((), (), s32[]{:S(2)}) async-start(), calls=%async_computation | async-start | bytes 1310720 | tf_op jit(solution)/shard_map/all_gather | solution.py:129
  9.1 47.8 %copy-start.3 = (bf16[256,512]{0,1:T(8,128)(2,1)S(1)}, bf16[256,512]{0,1:T(8,128)(2,1)}, u32[]{:S(2)}) copy-start(bf16[256,512]{0,1:T(8,128)(2,1)} %copy.80) | copy-start | bytes 786436
  9.1 106.3 %all-gather.6.cloned.1.call-start = ((), (), s32[]{:S(2)}) async-start(), calls=%async_computation.1 | async-start | bytes 2621440 | tf_op jit(solution)/shard_map/all_gather | solution.py:255
  11.4 14.0 %collective-permute-start.1 = (bf16[128,1024]{0,1:T(8,128)(2,1)S(1)}, bf16[128,1024]{0,1:T(8,128)(2,1)S(1)}, u32[]{:S(2)}, u32[]{:S(2)}) collective-permute-start(bf16[128,1024]{0,1:T(8,128)(2,1)S(1)} %get-tuple-element.421), channel_id=1, source_target_pairs={{4,0},{8,4},{12,8},{0,12},{5,1},{9,5},{13,9},{1,13},{6,2},{10,6},{... | collective-permute-start | bytes 786440 | tf_op jit(solution)/shard_map/ppermute | solution.py:34
  16.5 19.0 %collective-permute-start = (bf16[128,1024]{0,1:T(8,128)(2,1)S(1)}, bf16[128,1024]{0,1:T(8,128)(2,1)S(1)}, u32[]{:S(2)}, u32[]{:S(2)}) collective-permute-start(bf16[128,1024]{0,1:T(8,128)(2,1)S(1)} %get-tuple-element.420), channel_id=1, source_target_pairs={{0,4},{4,8},{8,12},{12,0},{1,5},{5,9},{9,13},{13,1},{2,6},{6,10},{... | collective-permute-start | bytes 786440 | tf_op jit(solution)/shard_map/ppermute | solution.py:33
  36.7 116.0 %all-gather.8.cloned.1.call-start = ((), (), s32[]{:S(2)}) async-start(), calls=%async_computation.2 | async-start | bytes 2621440 | tf_op jit(solution)/shard_map/all_gather | solution.py:256
  36.7 16.6 %collective-permute-start.2 = (bf16[256,512]{1,0:T(8,128)(2,1)S(1)}, bf16[256,512]{1,0:T(8,128)(2,1)S(1)}, u32[]{:S(2)}, u32[]{:S(2)}) collective-permute-start(bf16[256,512]{1,0:T(8,128)(2,1)S(1)} %copy-done.2), channel_id=1, source_target_pairs={{0,4},{4,8},{8,12},{12,0},{1,5},{5,9},{9,13},{13,1},{2,6},{6,10},{... | collective-permute-start | bytes 786440 | tf_op jit(solution)/shard_map/ppermute | solution.py:19
  39.3 24.9 %collective-permute-start.4 = (bf16[256,512]{1,0:T(8,128)(2,1)S(1)}, bf16[256,512]{1,0:T(8,128)(2,1)S(1)}, u32[]{:S(2)}, u32[]{:S(2)}) collective-permute-start(bf16[256,512]{1,0:T(8,128)(2,1)S(1)} %copy-done.2), channel_id=1, source_target_pairs={{0,12},{4,0},{8,4},{12,8},{1,13},{5,1},{9,5},{13,9},{2,14},{6,2},{... | collective-permute-start | bytes 786440 | tf_op jit(solution)/shard_map/ppermute | solution.py:21
  53.3 10.8 %collective-permute-start.3 = (bf16[256,512]{1,0:T(8,128)(2,1)S(1)}, bf16[256,512]{1,0:T(8,128)(2,1)S(1)}, u32[]{:S(2)}, u32[]{:S(2)}) collective-permute-start(bf16[256,512]{1,0:T(8,128)(2,1)S(1)} %collective-permute-done.2), channel_id=1, source_target_pairs={{0,4},{4,8},{8,12},{12,0},{1,5},{5,9},{9,13},{13,1},{2,6},{6,10},{... | collective-permute-start | bytes 786440 | tf_op jit(solution)/shard_map/ppermute | solution.py:19
  58.5 7.2 %copy-start.1 = (bf16[512,512]{0,1:T(8,128)(2,1)S(1)}, bf16[512,512]{0,1:T(8,128)(2,1)}, u32[]{:S(2)}) copy-start(bf16[512,512]{0,1:T(8,128)(2,1)} %get-tuple-element.419) | copy-start | bytes 1572868
  68.9 3.2 %copy-start = (f32[4,512,1024]{2,1,0:T(8,128)}, f32[4,512,1024]{2,1,0:T(8,128)S(1)}, u32[]{:S(2)}) copy-start(f32[4,512,1024]{2,1,0:T(8,128)S(1)} %get-tuple-element.426) | copy-start | bytes 25165828
  68.9 3.2 %copy-start.6 = (bf16[1024,512]{0,1:T(8,128)(2,1)S(1)}, bf16[1024,512]{0,1:T(8,128)(2,1)}, u32[]{:S(2)}) copy-start(bf16[1024,512]{0,1:T(8,128)(2,1)} %copy.83) | copy-start | bytes 3145732
  72.2 5.7 %copy-start.4 = (bf16[512,512]{0,1:T(8,128)(2,1)S(1)}, bf16[512,512]{0,1:T(8,128)(2,1)}, u32[]{:S(2)}) copy-start(bf16[512,512]{0,1:T(8,128)(2,1)} %get-tuple-element.418) | copy-start | bytes 1572868
  72.2 5.7 %copy-start.5 = (bf16[1024,512]{0,1:T(8,128)(2,1)S(1)}, bf16[1024,512]{0,1:T(8,128)(2,1)}, u32[]{:S(2)}) copy-start(bf16[1024,512]{0,1:T(8,128)(2,1)} %all-gather.4.cloned.1.call-done) | copy-start | bytes 3145732
  77.9 74.8 %copy-start.7 = (f32[256,4,128]{0,2,1:T(8,128)S(1)}, f32[256,4,128]{0,2,1:T(8,128)}, u32[]{:S(2)}) copy-start(f32[256,4,128]{0,2,1:T(8,128)} %custom-call) | copy-start | bytes 1572868
  77.9 74.8 %copy-start.8 = (f32[256,4,128]{0,2,1:T(8,128)S(1)}, f32[256,4,128]{0,2,1:T(8,128)}, u32[]{:S(2)}) copy-start(f32[256,4,128]{0,2,1:T(8,128)} %custom-call.1) | copy-start | bytes 1572868
Sparse Core Ops, SparseCore 0:
  10.2 48.4 all-gather.3
  60.2 46.1 all-gather.5
  108.0 44.6 all-gather.7
